TPU v7x, 1024 devices: a whole 8x8x8 slice. The times are simulated.
1024 devices in a mesh: expert: 16 (over y, core), dp: 64 (over z, x).
Axes of the slice: x: 8, y: 8, z: 8, core: 2. Of those that a mesh axis runs over, the one named last changes fastest.
Arguments:
- output_grad: bfloat16 [192, 7168], P('expert', 'dp'), may hold values from -6 to 6
- routing: int32 [192, 8], P('expert'), may hold values from 0 to 47, all different within a row; in each aligned block of 12 rows (0 to 11, 12 to 23, ...) at most 4 rows name the same one
- gates: float32 [192, 8], P('expert'), may hold values from 0.1 to 1
- saved_inputs: bfloat16 [48, 64, 7168], P('expert', None, 'dp'), may hold values from -6 to 6
- gate_up: bfloat16 [48, 7168, 2048], P('expert', 'dp'), may hold values from -0.0625 to 0.0625
- down_weight: bfloat16 [48, 1024, 7168], P('expert', None, 'dp'), may hold values from -0.0625 to 0.0625
Outputs:
- input_grad: bfloat16 [192, 7168], P('expert', 'dp')
- gate_up_grad: bfloat16 [48, 7168, 2048], P('expert', 'dp')
Inputs may be any that keep to these rules, and one draw needn't show every extreme that they name: `routing`: each token names 8 different experts. Among the routes of one block of 12 tokens no expert is named more than 4 times, a bound that some block reaches.
All inputs are finite; a program needn't handle non-finite values.
Results may differ from a plain program's by a relative error of at most 0.0064.
Values may be sent and summed in bfloat16 or wider, within the bound.
A program may use at most 32 MiB of HBM per device.

v0:
```python
import jax
import jax.numpy as jnp
from jax import lax
from jax.sharding import PartitionSpec as P


def body(output_grad, routing, gates, saved_inputs, gate_up, down_weight):
    tokens_here, top_count = routing.shape
    width_here = output_grad.shape[1]
    local_count = gate_up.shape[0]
    hidden_units = down_weight.shape[1]
    peer_count = lax.axis_size("expert")
    replica_count = lax.axis_size("dp")
    experts_all = local_count * peer_count
    slot_count = saved_inputs.shape[1]
    capacity = slot_count // peer_count
    units_here = hidden_units // replica_count
    flat_ids = routing.reshape(-1)
    expert_ids = jnp.arange(experts_all, dtype=jnp.int32)
    onehot = (flat_ids[:, None] == expert_ids[None, :]).astype(jnp.int32)
    earlier = jnp.cumsum(onehot, axis=0) - onehot
    rank_in = jnp.sum(earlier * onehot, axis=1)
    slot_id = flat_ids * capacity + rank_in
    slot_ids = jnp.arange(experts_all * capacity, dtype=jnp.int32)
    slot_table = (slot_id[:, None] == slot_ids[None, :]).astype(jnp.bfloat16)
    routed = (gates[:, :, None] * output_grad[:, None, :].astype(jnp.float32)).astype(jnp.bfloat16)
    routed = routed.reshape(tokens_here * top_count, width_here)
    outgoing = jnp.dot(slot_table.T, routed, preferred_element_type=jnp.float32).astype(
        jnp.bfloat16
    )
    outgoing = outgoing.reshape(experts_all, capacity, width_here)
    arrived = lax.all_to_all(outgoing, "expert", split_axis=0, concat_axis=0, tiled=True)
    arrived = arrived.reshape(peer_count, local_count, capacity, width_here)
    gate_cols = gate_up.reshape(local_count, width_here, 2, hidden_units)
    both = jnp.einsum("esd,edkf->fkes", saved_inputs, gate_cols, preferred_element_type=jnp.float32)
    hidden_part = jnp.einsum(
        "pecd,efd->fepc", arrived, down_weight, preferred_element_type=jnp.float32
    )
    hidden_part = hidden_part.reshape(hidden_units, 1, local_count, slot_count)
    shares = lax.psum_scatter(
        jnp.concatenate([both, hidden_part], axis=1).reshape(
            hidden_units, 3 * local_count * slot_count
        ),
        "dp",
        scatter_dimension=0,
        tiled=True,
    )
    shares = shares.reshape(units_here, 3, local_count, slot_count)
    gate_pre = shares[:, 0]
    up_pre = shares[:, 1]
    hidden_grad = shares[:, 2]
    sigmoid_gate = jax.nn.sigmoid(gate_pre)
    slope = sigmoid_gate * (1.0 + gate_pre * (1.0 - sigmoid_gate))
    pre_share = jnp.stack(
        [hidden_grad * up_pre * slope, hidden_grad * gate_pre * sigmoid_gate], axis=0
    ).astype(jnp.bfloat16)
    pre_grad = lax.all_gather(pre_share, "dp", axis=1, tiled=True)
    weight_grad = jnp.einsum(
        "esd,kfes->edkf", saved_inputs, pre_grad, preferred_element_type=jnp.float32
    )
    weight_grad = weight_grad.reshape(local_count, width_here, 2 * hidden_units).astype(
        jnp.bfloat16
    )
    pre_split = pre_grad.reshape(2, hidden_units, local_count, peer_count, capacity)
    slot_back = jnp.einsum(
        "kfepc,edkf->pecd", pre_split, gate_cols, preferred_element_type=jnp.float32
    ).astype(jnp.bfloat16)
    slot_back = slot_back.reshape(experts_all, capacity, width_here)
    returned_rows = lax.all_to_all(slot_back, "expert", split_axis=0, concat_axis=0, tiled=True)
    returned_rows = returned_rows.reshape(experts_all * capacity, width_here)
    token_grads = jnp.dot(slot_table, returned_rows, preferred_element_type=jnp.float32)
    input_grad = (
        token_grads.reshape(tokens_here, top_count, width_here).sum(axis=1).astype(jnp.bfloat16)
    )
    return (input_grad, weight_grad)


def solution(mesh):
    placed = (
        P("expert", "dp"),
        P("expert", None),
        P("expert", None),
        P("expert", None, "dp"),
        P("expert", "dp", None),
        P("expert", None, "dp"),
    )
    return jax.shard_map(
        body,
        mesh=mesh,
        in_specs=placed,
        out_specs=(P("expert", "dp"), P("expert", "dp", None)),
        check_vma=False,
    )
```

profile of v0, /device:TPU:1, one launch (start us, length us, event | category | flops | bytes accessed | tf_op | source)
XLA Modules:
  0.0 295.3 jit_solution(3163223867786812577)
XLA Ops:
  7.2 0.8 copy.36
  8.1 0.1 fusion.24
  8.2 0.1 reduce_window_sum.11
  8.3 0.2 select_reduce_fusion
  8.5 0.8 copy.39
  9.3 0.1 mul.101
  9.4 0.7 convert_element_type.35
  10.1 0.9 convolution_convert_fusion.1
  11.0 17.4 %all-to-all-start = ((bf16[48,4,112]{2,1,0:T(4,128)(2,1)}), bf16[48,4,112]{2,1,0:T(4,128)(2,1)S(1)}, u32[]{:S(2)}, u32[]{:S(2)}) async-start(bf16[48,4,112]{2,1,0:T(4,128)(2,1)} %bitcast.5), calls=%async_computation | async-start | bytes 98304 | tf_op jit(solution)/shard_map/all_to_all | solution.py:32
  28.5 1.7 convolution_bitcast_fusion
  30.2 5.7 %all-to-all-done = bf16[48,4,112]{2,1,0:T(4,128)(2,1)S(1)} async-done(((bf16[48,4,112]{2,1,0:T(4,128)(2,1)}), bf16[48,4,112]{2,1,0:T(4,128)(2,1)S(1)}, u32[]{:S(2)}, u32[]{:S(2)}) %all-to-all-start) | async-done | bytes 43040 | tf_op jit(solution)/shard_map/all_to_all | solution.py:32
  35.9 0.3 convolution_bitcast_fusion.1
  36.2 1.4 copy.41
  37.6 1.4 reshape.158
  39.0 0.3 pad_maximum_fusion
  39.3 1.6 copy.42
  40.9 1.3 copy-done.1
  42.2 1.9 reshape.155
  44.1 1.3 dynamic-slice
  46.0 166.6 %all-reduce.3.cloned.1.call-done = f32[1024,576]{0,1:T(8,128)} async-done(((f32[1024,576]{0,1:T(8,128)}), f32[1024,576]{0,1:T(8,128)}) %all-reduce.3.cloned.1.call-update) | async-done | bytes 2359312
  212.7 1.1 constant_dynamic-slice_fusion
  213.9 0.1 copy.65
  214.0 0.1 copy.66
  214.1 39.3 %all_gather.3 = bf16[2,1024,3,64]{3,1,0,2:T(8,128)(2,1)S(1)} all-gather(bf16[2,16,3,64]{3,1,0,2:T(8,128)(2,1)S(1)} %pad_maximum_fusion.1), channel_id=1, replica_groups=mesh['expert'=16,'dp'=64] {'dp'}, dimensions={1}, use_global_device_ids=true | all-gather | bytes 798720 | tf_op jit(solution)/shard_map/all_gather | solution.py:57
  253.5 0.9 copy.47
  254.4 2.4 fusion.11
  256.8 0.6 copy.50
  257.5 22.7 %all-to-all-start.1 = ((bf16[48,4,112]{2,1,0:T(4,128)(2,1)}), bf16[48,4,112]{2,1,0:T(4,128)(2,1)S(1)}, u32[]{:S(2)}, u32[]{:S(2)}) async-start(bf16[48,4,112]{2,1,0:T(4,128)(2,1)} %bitcast.20), calls=%async_computation.1 | async-start | bytes 98304 | tf_op jit(solution)/shard_map/all_to_all | solution.py:69
  280.2 0.6 fusion
  280.8 1.2 copy.68
  282.0 5.7 %all-to-all-done.1 = bf16[48,4,112]{2,1,0:T(4,128)(2,1)S(1)} async-done(((bf16[48,4,112]{2,1,0:T(4,128)(2,1)}), bf16[48,4,112]{2,1,0:T(4,128)(2,1)S(1)}, u32[]{:S(2)}, u32[]{:S(2)}) %all-to-all-start.1) | async-done | bytes 43040 | tf_op jit(solution)/shard_map/all_to_all | solution.py:69
  287.7 0.8 convolution_reduce_fusion
  (15 shorter events, 0.4 us)
Async XLA Ops:
  7.2 28.8 %copy-start = (bf16[3,1024,112]{1,2,0:T(8,128)(2,1)S(1)}, bf16[3,1024,112]{1,2,0:T(8,128)(2,1)}, u32[]{:S(2)}) copy-start(bf16[3,1024,112]{1,2,0:T(8,128)(2,1)} %param.11) | copy-start | bytes 2064388
  11.0 25.0 %all-to-all-start = ((bf16[48,4,112]{2,1,0:T(4,128)(2,1)}), bf16[48,4,112]{2,1,0:T(4,128)(2,1)S(1)}, u32[]{:S(2)}, u32[]{:S(2)}) async-start(bf16[48,4,112]{2,1,0:T(4,128)(2,1)} %bitcast.5), calls=%async_computation | async-start | bytes 98304 | tf_op jit(solution)/shard_map/all_to_all | solution.py:32
  28.4 184.2 %all-reduce.3.cloned.1.call-start = ((), (), s32[]{:S(2)}) async-start(), calls=%async_computation.2 | async-start | bytes 4718592
  40.8 1.3 copy-start.1
  254.4 25.8 %copy-start.2 = (bf16[3,64,112]{2,1,0:T(8,128)(2,1)S(1)}, bf16[3,64,112]{2,1,0:T(8,128)(2,1)}, u32[]{:S(2)}) copy-start(bf16[3,64,112]{2,1,0:T(8,128)(2,1)} %param.9) | copy-start | bytes 129028
  257.5 30.2 %all-to-all-start.1 = ((bf16[48,4,112]{2,1,0:T(4,128)(2,1)}), bf16[48,4,112]{2,1,0:T(4,128)(2,1)S(1)}, u32[]{:S(2)}, u32[]{:S(2)}) async-start(bf16[48,4,112]{2,1,0:T(4,128)(2,1)} %bitcast.20), calls=%async_computation.1 | async-start | bytes 98304 | tf_op jit(solution)/shard_map/all_to_all | solution.py:69
Sparse Core Ops, SparseCore 0:
  41.0 171.6 all-reduce.2
where the time goes:
time: 296 us; the launch traced here: 295 us
  waiting for transfers between devices  178 us (60%)
  starting transfers between devices  40.2 us (14%)
  blocking collectives  39.3 us (13%)
  local copies, waits for them, and re-layouts  14.8 us (5%)
  between operations  14.8 us (5%)
  matrix products  6.74 us (2%)
    unnamed x2, waiting for transfers between devices  167 us
    all_gather x1, blocking collectives, body(): pre_grad = lax.all_gather(pre_share, 'dp', axis=1, tiled=True)  39.3 us
    all_to_all x1, starting transfers between devices, body(): lax.all_to_all(slot_back, 'expert', split_axis=0, concat_axis=0, tiled=True)  22.7 us
    all_to_all x1, starting transfers between devices, body(): lax.all_to_all(outgoing, 'expert', split_axis=0, concat_axis=0, tiled=True)  17.4 us
  transfers between devices with their start and end apart: 3, of which 3 were waited for; matrix products, arithmetic and copies ran while one was open for 2% of the time, Pallas kernels for 0%

commit v1 on v0

v1 whole, which is shorter than its diff:
```python
import jax
import jax.numpy as jnp
from jax import lax
from jax.experimental import pallas as pl
from jax.experimental.pallas import tpu as pltpu
from jax.sharding import PartitionSpec as P

BF16 = jnp.bfloat16
F32 = jnp.float32
SIDE = 8
PEERS = 16
MINE = 3
SLOTS = 64
TILE = 256


def kernel(
    og_ref, rt_ref, gt_ref, x_ref, w_ref, d_ref,
    ig_ref, wg_ref,
    og_pad, rt_pad, gt_pad, table,
    e1_send, e1_recv, got, gu_send, gu_recv, h_send, h_recv, s2_send, s2_recv,
    gath, pre, slot_rows, e2_send, e2_recv,
    e_sems, r_sems, s_sems,
):
    ex = lax.axis_index("expert")
    dp = lax.axis_index("dp")
    z = dp // SIDE
    x = dp % SIDE
    even = ex % 2 == 0
    first = jnp.where(even, x, z)
    second = jnp.where(even, z, x)
    first_step = jnp.where(even, 1, SIDE)
    second_step = jnp.where(even, SIDE, 1)

    def along_first(k):
        to = (first + k) % SIDE
        return (ex, dp + (to - first) * first_step), to

    def along_second(k):
        to = (second + k) % SIDE
        return (ex, dp + (to - second) * second_step), to

    def along_expert(k):
        to = (ex + k) % PEERS
        return (to, dp), to

    barrier = pltpu.get_barrier_semaphore()

    def greet(who, count):
        @pl.loop(1, count)
        def _(k):
            pl.semaphore_signal(
                barrier, inc=1, device_id=who(k)[0], device_id_type=pl.DeviceIdType.MESH
            )

    greet(along_first, SIDE)
    greet(along_second, SIDE)
    greet(along_expert, PEERS)

    def send(src, dst, send_sem, recv_sem, device):
        pltpu.make_async_remote_copy(
            src_ref=src, dst_ref=dst, send_sem=send_sem, recv_sem=recv_sem,
            device_id=device, device_id_type=pl.DeviceIdType.MESH,
        ).start()

    def wait(ref, sem):
        pltpu.make_async_copy(ref, ref, sem).wait()

    og_pad[...] = jnp.zeros_like(og_pad)
    og_pad[0:12, 0:112] = og_ref[...]
    rt_pad[...] = jnp.full_like(rt_pad, -2)
    rt_pad[:, 0:12] = rt_ref[...]
    gt_pad[...] = jnp.zeros_like(gt_pad)
    gt_pad[:, 0:12] = gt_ref[...]
    shape = (PEERS * 16, 128)
    row = lax.broadcasted_iota(jnp.int32, shape, 0)
    which = (row >> 2) & 3
    expert_id = jnp.where(which < MINE, (row >> 4) * MINE + which, -1)
    names = jnp.zeros(shape, F32)
    gate = jnp.zeros(shape, F32)
    for k in range(8):
        hit = rt_pad[k : k + 1, :] == expert_id
        names = names + jnp.where(hit, 1.0, 0.0)
        gate = gate + jnp.where(hit, gt_pad[k : k + 1, :], 0.0)
    before = lax.broadcasted_iota(jnp.int32, (128, 128), 0) < lax.broadcasted_iota(
        jnp.int32, (128, 128), 1
    )
    rank = jnp.dot(
        names.astype(BF16), jnp.where(before, 1.0, 0.0).astype(BF16), preferred_element_type=F32
    )
    fills = jnp.where(rank == (row & 3).astype(F32), names, 0.0)
    gate_of = jnp.sum(fills * gate, axis=1, keepdims=True)
    table[...] = fills.astype(BF16)
    rows_out = jnp.dot(table[...], og_pad[...], preferred_element_type=F32) * gate_of
    e1_send[...] = rows_out.astype(BF16).reshape(PEERS, 16, 128)

    for e in range(MINE):
        for n in range(2048 // TILE):
            part = jnp.dot(
                x_ref[e], w_ref[e, :, n * TILE : (n + 1) * TILE], preferred_element_type=F32
            ).astype(BF16)
            kind, at = divmod(n * TILE, 1024)
            for i in range(TILE // 128):
                gu_send[at // 128 + i, e, kind * SLOTS : (kind + 1) * SLOTS, :] = part[
                    :, i * 128 : (i + 1) * 128
                ]

    pl.semaphore_wait(barrier, 2 * (SIDE - 1) + PEERS - 1)

    @pl.loop(1, PEERS)
    def _(k):
        device, to = along_expert(k)
        send(e1_send.at[to], e1_recv.at[ex], e_sems.at[0], e_sems.at[1], device)

    e1_recv[ex] = e1_send[ex]

    for e in range(MINE):

        @pl.loop(1, SIDE)
        def _(k):
            device, to = along_first(k)
            send(gu_send.at[to, e], gu_recv.at[e, k - 1], s_sems.at[0, e], r_sems.at[0, e], device)

    wait(e1_recv.at[0 : PEERS - 1], e_sems.at[1])
    take = lax.broadcasted_iota(jnp.int32, (MINE * SLOTS, 256), 0)
    lane = lax.broadcasted_iota(jnp.int32, (MINE * SLOTS, 256), 1)
    source = ((take >> 2) & 15) * 16 + (take >> 6) * 4 + (take & 3)
    pick = jnp.where(lane == source, 1.0, 0.0).astype(BF16)
    got[...] = jnp.dot(
        pick, e1_recv[...].reshape(PEERS * 16, 128), preferred_element_type=F32
    ).astype(BF16)
    for e in range(MINE):
        for n in range(1024 // TILE):
            part = jnp.dot(
                got[e * SLOTS : (e + 1) * SLOTS, 0:112],
                d_ref[e, :, n * TILE : (n + 1) * TILE],
                preferred_element_type=F32,
            ).astype(BF16)
            for i in range(TILE // 128):
                h_send[n * TILE // 128 + i, e] = part[:, i * 128 : (i + 1) * 128]

        @pl.loop(1, SIDE)
        def _(k):
            device, to = along_first(k)
            send(h_send.at[to, e], h_recv.at[e, k - 1], s_sems.at[1, e], r_sems.at[1, e], device)

    for e in range(MINE):
        wait(gu_recv.at[e], r_sems.at[0, e])
        total = gu_send[first, e].astype(F32)
        for k in range(SIDE - 1):
            total = total + gu_recv[e, k].astype(F32)
        s2_send[:, e, 0:8, :] = total[0:SLOTS].reshape(SIDE, 8, 128)
        s2_send[:, e, 8:16, :] = total[SLOTS:].reshape(SIDE, 8, 128)
        wait(h_recv.at[e], r_sems.at[1, e])
        total = h_send[first, e].astype(F32)
        for k in range(SIDE - 1):
            total = total + h_recv[e, k].astype(F32)
        s2_send[:, e, 16:24, :] = total.reshape(SIDE, 8, 128)

        @pl.loop(1, SIDE)
        def _(k):
            device, to = along_second(k)
            send(s2_send.at[to, e], s2_recv.at[e, k - 1], s_sems.at[2, e], r_sems.at[2, e], device)

    for e in range(MINE):
        wait(s2_recv.at[e], r_sems.at[2, e])
        total = s2_send[second, e]
        for k in range(SIDE - 1):
            total = total + s2_recv[e, k]
        gate_pre, up_pre, hidden = total[0:8], total[8:16], total[16:24]
        sg = 1.0 / (1.0 + jnp.exp(-gate_pre))
        slope = sg * (1.0 + gate_pre * (1.0 - sg))
        both = jnp.concatenate([hidden * up_pre * slope, hidden * gate_pre * sg], axis=0)
        gath[e, first, second] = both.astype(BF16)

        @pl.loop(1, SIDE)
        def _(k):
            device, _to = along_second(k)
            here = gath.at[e, first, second]
            send(here, here, s_sems.at[3, e], r_sems.at[3, e], device)

    for e in range(MINE):
        wait(gath.at[e, 0, 0 : SIDE - 1], r_sems.at[3, e])

        @pl.loop(1, SIDE)
        def _(k):
            device, _to = along_first(k)
            here = gath.at[e, first]
            send(here, here, s_sems.at[4, e], r_sems.at[4, e], device)

    slot_rows[...] = jnp.zeros_like(slot_rows)
    for e in range(MINE):
        wait(gath.at[e, 0 : SIDE - 1], r_sems.at[4, e])
        for j in range(SIDE):
            block = gath[e, j].astype(F32)
            pre[e, :, j * 128 : (j + 1) * 128] = block[:, 0:8].reshape(SLOTS, 128).astype(BF16)
            pre[e, :, 1024 + j * 128 : 1024 + (j + 1) * 128] = (
                block[:, 8:16].reshape(SLOTS, 128).astype(BF16)
            )
        slot_rows[e * SLOTS : (e + 1) * SLOTS, 0:112] = lax.dot_general(
            pre[e], w_ref[e], (((1,), (1,)), ((), ())), preferred_element_type=F32
        ).astype(BF16)
    back = lax.broadcasted_iota(jnp.int32, (256, 256), 0)
    lane = lax.broadcasted_iota(jnp.int32, (256, 256), 1)
    source = jnp.where(
        ((back >> 2) & 3) < MINE, ((back >> 2) & 3) * SLOTS + (back >> 4) * 4 + (back & 3), -1
    )
    e2_send[...] = (
        jnp.dot(
            jnp.where(lane == source, 1.0, 0.0).astype(BF16),
            slot_rows[...],
            preferred_element_type=F32,
        )
        .astype(BF16)
        .reshape(PEERS, 16, 128)
    )

    @pl.loop(1, PEERS)
    def _(k):
        device, to = along_expert(k)
        send(e2_send.at[to], e2_recv.at[ex], e_sems.at[2], e_sems.at[3], device)

    e2_recv[ex] = e2_send[ex]

    for e in range(MINE):
        for n in range(2048 // TILE):
            cols = slice(n * TILE, (n + 1) * TILE)
            wg_ref[e, :, cols] = lax.dot_general(
                x_ref[e], pre[e, :, cols], (((0,), (0,)), ((), ())), preferred_element_type=F32
            ).astype(BF16)

    wait(e2_recv.at[0 : PEERS - 1], e_sems.at[3])
    token = lax.dot_general(
        table[...],
        e2_recv[...].reshape(PEERS * 16, 128),
        (((0,), (0,)), ((), ())),
        preferred_element_type=F32,
    )
    ig_ref[...] = token[0:12, 0:112].astype(BF16)

    wait(e1_send.at[0 : PEERS - 1], e_sems.at[0])
    wait(e2_send.at[0 : PEERS - 1], e_sems.at[2])
    for e in range(MINE):
        wait(gu_recv.at[e], s_sems.at[0, e])
        wait(h_recv.at[e], s_sems.at[1, e])
        wait(s2_recv.at[e], s_sems.at[2, e])
        wait(gath.at[e, 0, 0 : SIDE - 1], s_sems.at[3, e])
        wait(gath.at[e, 0 : SIDE - 1], s_sems.at[4, e])


def body(output_grad, routing, gates, saved_inputs, gate_up, down_weight):
    vmem = pl.BlockSpec(memory_space=pltpu.VMEM)
    dma = pltpu.SemaphoreType.DMA
    return pl.pallas_call(
        kernel,
        out_shape=(
            jax.ShapeDtypeStruct(output_grad.shape, BF16),
            jax.ShapeDtypeStruct(gate_up.shape, BF16),
        ),
        in_specs=[vmem] * 6,
        out_specs=(vmem, vmem),
        scratch_shapes=[
            pltpu.VMEM((128, 128), BF16),
            pltpu.VMEM((8, 128), jnp.int32),
            pltpu.VMEM((8, 128), F32),
            pltpu.VMEM((256, 128), BF16),
            pltpu.VMEM((PEERS, 16, 128), BF16),
            pltpu.VMEM((PEERS, 16, 128), BF16),
            pltpu.VMEM((MINE * SLOTS, 128), BF16),
            pltpu.VMEM((SIDE, MINE, 2 * SLOTS, 128), BF16),
            pltpu.VMEM((MINE, SIDE - 1, 2 * SLOTS, 128), BF16),
            pltpu.VMEM((SIDE, MINE, SLOTS, 128), BF16),
            pltpu.VMEM((MINE, SIDE - 1, SLOTS, 128), BF16),
            pltpu.VMEM((SIDE, MINE, 24, 128), F32),
            pltpu.VMEM((MINE, SIDE - 1, 24, 128), F32),
            pltpu.VMEM((MINE, SIDE, SIDE, 16, 128), BF16),
            pltpu.VMEM((MINE, SLOTS, 2048), BF16),
            pltpu.VMEM((256, 128), BF16),
            pltpu.VMEM((PEERS, 16, 128), BF16),
            pltpu.VMEM((PEERS, 16, 128), BF16),
            dma((4,)),
            dma((5, MINE)),
            dma((5, MINE)),
        ],
        compiler_params=pltpu.CompilerParams(
            collective_id=1, has_side_effects=True, vmem_limit_bytes=48 << 20
        ),
    )(
        output_grad,
        routing.T,
        gates.T,
        saved_inputs,
        gate_up,
        jnp.swapaxes(down_weight, 1, 2),
    )


def solution(mesh):
    placed = (
        P("expert", "dp"),
        P("expert", None),
        P("expert", None),
        P("expert", None, "dp"),
        P("expert", "dp", None),
        P("expert", None, "dp"),
    )
    return jax.shard_map(
        body,
        mesh=mesh,
        in_specs=placed,
        out_specs=(P("expert", "dp"), P("expert", "dp", None)),
        check_vma=False,
    )
```

time: 296 us -> 74.6 us (0.25)
  waiting for transfers between devices: 178 us -> 0 us
  Pallas kernels: 0 us -> 66.6 us
  starting transfers between devices: 40.2 us -> 0 us
  blocking collectives: 39.3 us -> 0 us
  between operations: 14.8 us -> 0.65 us
  local copies, waits for them, and re-layouts: 14.8 us -> 6.96 us
  matrix products: 6.74 us -> 0 us
    unnamed x2 -> x0, waiting for transfers between devices: 167 us -> none
    pallas_call x0 -> x1, Pallas kernels: none -> 66.6 us  [body(): pl.pallas_call(kernel, out_shape=(jax.ShapeDtypeStruct(output_grad.shape,...]
    all_to_all x2 -> x0, starting transfers between devices: 40.1 us -> none  [the longest x1 22.7 us: body(): lax.all_to_all(slot_back, 'expert', split_axis=0, concat_axis=0, tiled=True)]
    all_gather x1 -> x0, blocking collectives: 39.3 us -> none  [body(): pre_grad = lax.all_gather(pre_share, 'dp', axis=1, tiled=True)]
    all_to_all x2 -> x0, waiting for transfers between devices: 11.4 us -> none  [the longest x1 5.74 us: body(): lax.all_to_all(outgoing, 'expert', split_axis=0, concat_axis=0, tiled=True)]
    dot_general x6 -> x0, matrix products: 6.74 us -> none  [the longest x1 2.44 us: body(): jnp.einsum('kfepc,edkf->pecd', pre_split, gate_cols, preferred_element_ty...]
    reshape x2 -> x0, local copies, waits for them, and re-layouts: 3.26 us -> none  [the longest x1 1.86 us: body(): gate_cols = gate_up.reshape(local_count, width_here, 2, hidden_units)]
    unnamed x13 -> x14, local copies, waits for them, and re-layouts: 5.54 us -> 6.96 us
  transfers between devices with their start and end apart: 3 -> 0, of which waited for: 3 -> 0; matrix products, arithmetic and copies ran while one was open for 2% -> 0% of each run, Pallas kernels for 0% -> 0%
where the time goes in v1:
time: 74.6 us; the launch traced here: 74.3 us
  Pallas kernels  66.6 us (89%)
  local copies, waits for them, and re-layouts  6.96 us (9%)
    pallas_call x1, Pallas kernels, body(): pl.pallas_call(kernel, out_shape=(jax.ShapeDtypeStruct(output_grad.shape,...  66.6 us
    unnamed x14, local copies, waits for them, and re-layouts  6.96 us

profile of v1, /device:TPU:1, one launch (start us, length us, event | category | flops | bytes accessed | tf_op | source)
XLA Modules:
  0.0 74.3 jit_solution(12372245741913241175)
XLA Ops:
  0.6 0.0 copy-start
  0.6 1.3 %copy-done = bf16[3,112,2048]{2,1,0:T(8,128)(2,1)S(1)} copy-done((bf16[3,112,2048]{2,1,0:T(8,128)(2,1)S(1)}, bf16[3,112,2048]{2,1,0:T(8,128)(2,1)}, u32[]{:S(2)}) %copy-start) | copy-done | bytes 1376280
  2.0 0.0 copy-start.1
  2.0 1.1 %copy-done.1 = bf16[3,1024,112]{1,2,0:T(8,128)(2,1)S(1)} copy-done((bf16[3,1024,112]{1,2,0:T(8,128)(2,1)S(1)}, bf16[3,1024,112]{1,2,0:T(8,128)(2,1)}, u32[]{:S(2)}) %copy-start.1) | copy-done | bytes 688152
  3.1 0.0 copy-start.2
  3.1 0.8 %copy-done.2 = bf16[3,64,112]{2,1,0:T(8,128)(2,1)S(1)} copy-done((bf16[3,64,112]{2,1,0:T(8,128)(2,1)S(1)}, bf16[3,64,112]{2,1,0:T(8,128)(2,1)}, u32[]{:S(2)}) %copy-start.2) | copy-done | bytes 43032
  3.9 0.0 copy-start.3
  3.9 0.7 copy-done.3
  4.6 0.0 copy-start.4
  4.6 0.7 copy-done.4
  5.2 0.0 copy-start.5
  5.2 0.7 copy-done.5
  5.9 66.6 %shard_map.77 = (bf16[12,112]{1,0:T(8,128)(2,1)S(1)}, bf16[3,112,2048]{2,1,0:T(8,128)(2,1)S(1)}) custom-call(bf16[12,112]{1,0:T(8,128)(2,1)S(1)} %copy-done.3, s32[8,12]{1,0:T(8,128)S(1)} %bitcast.4, f32[8,12]{1,0:T(8,128)S(1)} %bitcast.5, bf16[3,64,112]{2,1,0:T(8,128)(2,1)S(1)} %copy-done.2, bf16[3,112,2048]{2,1,0:T(8,128)(2,1)S(1)} %copy-done, ...), custom_call_target="tpu_custom_call" | custom-call | tf_op jit(solution)/shard_map/pallas_call | solution.py:254
  72.6 0.6 copy.10
  73.2 1.1 %copy.11 = bf16[3,112,2048]{2,1,0:T(8,128)(2,1)} copy(bf16[3,112,2048]{2,1,0:T(8,128)(2,1)S(1)} %get-tuple-element.5) | data formatting | bytes 2752512
Async XLA Ops:
  0.6 1.3 %copy-start = (bf16[3,112,2048]{2,1,0:T(8,128)(2,1)S(1)}, bf16[3,112,2048]{2,1,0:T(8,128)(2,1)}, u32[]{:S(2)}) copy-start(bf16[3,112,2048]{2,1,0:T(8,128)(2,1)} %w_ref.1) | copy-start | bytes 4128772
  2.0 1.1 %copy-start.1 = (bf16[3,1024,112]{1,2,0:T(8,128)(2,1)S(1)}, bf16[3,1024,112]{1,2,0:T(8,128)(2,1)}, u32[]{:S(2)}) copy-start(bf16[3,1024,112]{1,2,0:T(8,128)(2,1)} %param.11) | copy-start | bytes 2064388
  3.1 0.8 %copy-start.2 = (bf16[3,64,112]{2,1,0:T(8,128)(2,1)S(1)}, bf16[3,64,112]{2,1,0:T(8,128)(2,1)}, u32[]{:S(2)}) copy-start(bf16[3,64,112]{2,1,0:T(8,128)(2,1)} %x_ref.1) | copy-start | bytes 129028
  3.9 0.7 copy-start.3
  4.6 0.7 copy-start.4
  5.2 0.7 copy-start.5

commit v2 on v1

--- a/solution.py
+++ b/solution.py
@@ -15,12 +15,14 @@
 
 
 def kernel(
-    og_ref, rt_ref, gt_ref, x_ref, w_ref, d_ref,
-    ig_ref, wg_ref,
+    og_hbm, rt_hbm, gt_hbm, x_hbm, w_hbm, d_hbm,
+    ig_hbm, wg_hbm,
+    ig_ref, wg_ref, out_sems,
+    og_ref, rt_ref, gt_ref, x_ref, w_ref, d_ref, in_sems,
     og_pad, rt_pad, gt_pad, table,
-    e1_send, e1_recv, got, gu_send, gu_recv, h_send, h_recv, s2_send, s2_recv,
+    e1_send, e1_recv, got, gu_send, gu_recv, far3, far4, passed, h_send, h_recv, s2_send, s2_recv,
     gath, pre, slot_rows, e2_send, e2_recv,
-    e_sems, r_sems, s_sems,
+    e_sems, r_sems, s_sems, ready,
 ):
     ex = lax.axis_index("expert")
     dp = lax.axis_index("dp")
@@ -53,9 +55,39 @@
                 barrier, inc=1, device_id=who(k)[0], device_id_type=pl.DeviceIdType.MESH
             )
 
-    greet(along_first, SIDE)
-    greet(along_second, SIDE)
+    loads = {
+        "x": (x_hbm, x_ref), "w0": (w_hbm.at[0], w_ref.at[0]), "w1": (w_hbm.at[1], w_ref.at[1]),
+        "w2": (w_hbm.at[2], w_ref.at[2]), "og": (og_hbm, og_ref), "rt": (rt_hbm, rt_ref),
+        "gt": (gt_hbm, gt_ref), "d": (d_hbm, d_ref),
+    }
+    loads = {
+        name: pltpu.make_async_copy(src, dst, in_sems.at[i])
+        for i, (name, (src, dst)) in enumerate(loads.items())
+    }
+    for load in loads.values():
+        load.start()
+    def along_x(k):
+        to = (x + k) % SIDE
+        return (ex, z * SIDE + to), to
+
+    def at_z(to):
+        return (ex, to * SIDE + x)
+
     greet(along_expert, PEERS)
+    greet(along_x, SIDE)
+
+    @pl.loop(z + 1, SIDE)
+    def _(to):
+        pl.semaphore_signal(
+            barrier, inc=1, device_id=at_z(to), device_id_type=pl.DeviceIdType.MESH
+        )
+
+    def await_ready(k, turn):
+        to = (z + k) % SIDE
+
+        @pl.when(jnp.logical_and(turn, to > z))
+        def _():
+            pl.semaphore_wait(ready.at[to], 1)
 
     def send(src, dst, send_sem, recv_sem, device):
         pltpu.make_async_remote_copy(
@@ -66,6 +98,21 @@
     def wait(ref, sem):
         pltpu.make_async_copy(ref, ref, sem).wait()
 
+    loads["x"].wait()
+    for e in range(MINE):
+        loads[f"w{e}"].wait()
+        for n in range(2048 // TILE):
+            part = jnp.dot(
+                x_ref[e], w_ref[e, :, n * TILE : (n + 1) * TILE], preferred_element_type=F32
+            ).astype(BF16)
+            kind, at = divmod(n * TILE, 1024)
+            for i in range(TILE // 128):
+                gu_send[at // 128 + i, e, kind * SLOTS : (kind + 1) * SLOTS, :] = part[
+                    :, i * 128 : (i + 1) * 128
+                ]
+
+    for name in ("og", "rt", "gt"):
+        loads[name].wait()
     og_pad[...] = jnp.zeros_like(og_pad)
     og_pad[0:12, 0:112] = og_ref[...]
     rt_pad[...] = jnp.full_like(rt_pad, -2)
@@ -94,18 +141,13 @@
     rows_out = jnp.dot(table[...], og_pad[...], preferred_element_type=F32) * gate_of
     e1_send[...] = rows_out.astype(BF16).reshape(PEERS, 16, 128)
 
-    for e in range(MINE):
-        for n in range(2048 // TILE):
-            part = jnp.dot(
-                x_ref[e], w_ref[e, :, n * TILE : (n + 1) * TILE], preferred_element_type=F32
-            ).astype(BF16)
-            kind, at = divmod(n * TILE, 1024)
-            for i in range(TILE // 128):
-                gu_send[at // 128 + i, e, kind * SLOTS : (kind + 1) * SLOTS, :] = part[
-                    :, i * 128 : (i + 1) * 128
-                ]
-
-    pl.semaphore_wait(barrier, 2 * (SIDE - 1) + PEERS - 1)
+    pl.semaphore_wait(barrier, SIDE - 1 + PEERS - 1 + z)
+
+    @pl.loop(0, z)
+    def _(to):
+        pl.semaphore_signal(
+            ready.at[z], inc=1, device_id=at_z(to), device_id_type=pl.DeviceIdType.MESH
+        )
 
     @pl.loop(1, PEERS)
     def _(k):
@@ -114,13 +156,38 @@
 
     e1_recv[ex] = e1_send[ex]
 
-    for e in range(MINE):
-
-        @pl.loop(1, SIDE)
-        def _(k):
-            device, to = along_first(k)
-            send(gu_send.at[to, e], gu_recv.at[e, k - 1], s_sems.at[0, e], r_sems.at[0, e], device)
-
+    odd = jnp.logical_not(even)
+    for side, way in ((1, 1), (0, -1)):
+        one, next_one = along_first(way)
+        two, _ = along_first(2 * way)
+        _, third = along_first(3 * way)
+        _, fourth = along_first(4)
+        half = pl.ds(side * SLOTS, SLOTS)
+        await_ready(way, odd)
+        for e in range(MINE):
+            send(gu_send.at[third, e], far3.at[e, side], s_sems.at[5, e], r_sems.at[5, e], one)
+        await_ready(2 * way, odd)
+        for e in range(MINE):
+            send(
+                gu_send.at[fourth, e, half], far4.at[e, side],
+                s_sems.at[6, e], r_sems.at[6, e], two,
+            )
+        for e in range(MINE):
+            send(gu_send.at[next_one, e], gu_recv.at[e, side], s_sems.at[0, e], r_sems.at[0, e], one)
+    for e in range(MINE):
+        wait(far3.at[e], r_sems.at[5, e])
+        wait(far4.at[e], r_sems.at[6, e])
+        for side, way in enumerate((-1, 1)):
+            two, second_one = along_first(2 * way)
+            total = gu_send[second_one, e].astype(F32) + far3[e, side].astype(F32)
+            extra = far4[e, side].astype(F32)
+            parts = [total[0:SLOTS], total[SLOTS:]]
+            parts[side] = parts[side] + extra
+            passed[e, side, 0:SLOTS] = parts[0].astype(BF16)
+            passed[e, side, SLOTS:] = parts[1].astype(BF16)
+            send(passed.at[e, side], gu_recv.at[e, 2 + side], s_sems.at[0, e], r_sems.at[0, e], two)
+
+    loads["d"].wait()
     wait(e1_recv.at[0 : PEERS - 1], e_sems.at[1])
     take = lax.broadcasted_iota(jnp.int32, (MINE * SLOTS, 256), 0)
     lane = lax.broadcasted_iota(jnp.int32, (MINE * SLOTS, 256), 1)
@@ -129,6 +196,8 @@
     got[...] = jnp.dot(
         pick, e1_recv[...].reshape(PEERS * 16, 128), preferred_element_type=F32
     ).astype(BF16)
+    for k in (3, 4, 5):
+        await_ready(k, odd)
     for e in range(MINE):
         for n in range(1024 // TILE):
             part = jnp.dot(
@@ -144,10 +213,12 @@
             device, to = along_first(k)
             send(h_send.at[to, e], h_recv.at[e, k - 1], s_sems.at[1, e], r_sems.at[1, e], device)
 
+    for k in range(1, SIDE):
+        await_ready(k, even)
     for e in range(MINE):
         wait(gu_recv.at[e], r_sems.at[0, e])
         total = gu_send[first, e].astype(F32)
-        for k in range(SIDE - 1):
+        for k in range(4):
             total = total + gu_recv[e, k].astype(F32)
         s2_send[:, e, 0:8, :] = total[0:SLOTS].reshape(SIDE, 8, 128)
         s2_send[:, e, 8:16, :] = total[SLOTS:].reshape(SIDE, 8, 128)
@@ -228,6 +299,7 @@
             wg_ref[e, :, cols] = lax.dot_general(
                 x_ref[e], pre[e, :, cols], (((0,), (0,)), ((), ())), preferred_element_type=F32
             ).astype(BF16)
+        pltpu.make_async_copy(wg_ref.at[e], wg_hbm.at[e], out_sems.at[e]).start()
 
     wait(e2_recv.at[0 : PEERS - 1], e_sems.at[3])
     token = lax.dot_general(
@@ -237,11 +309,18 @@
         preferred_element_type=F32,
     )
     ig_ref[...] = token[0:12, 0:112].astype(BF16)
-
+    last = pltpu.make_async_copy(ig_ref, ig_hbm, out_sems.at[MINE])
+    last.start()
+
+    for e in range(MINE):
+        pltpu.make_async_copy(wg_ref.at[e], wg_hbm.at[e], out_sems.at[e]).wait()
+    last.wait()
     wait(e1_send.at[0 : PEERS - 1], e_sems.at[0])
     wait(e2_send.at[0 : PEERS - 1], e_sems.at[2])
     for e in range(MINE):
         wait(gu_recv.at[e], s_sems.at[0, e])
+        wait(far3.at[e], s_sems.at[5, e])
+        wait(far4.at[e], s_sems.at[6, e])
         wait(h_recv.at[e], s_sems.at[1, e])
         wait(s2_recv.at[e], s_sems.at[2, e])
         wait(gath.at[e, 0, 0 : SIDE - 1], s_sems.at[3, e])
@@ -249,7 +328,6 @@
 
 
 def body(output_grad, routing, gates, saved_inputs, gate_up, down_weight):
-    vmem = pl.BlockSpec(memory_space=pltpu.VMEM)
     dma = pltpu.SemaphoreType.DMA
     return pl.pallas_call(
         kernel,
@@ -257,9 +335,19 @@
             jax.ShapeDtypeStruct(output_grad.shape, BF16),
             jax.ShapeDtypeStruct(gate_up.shape, BF16),
         ),
-        in_specs=[vmem] * 6,
-        out_specs=(vmem, vmem),
+        in_specs=[pl.BlockSpec(memory_space=pl.ANY)] * 6,
+        out_specs=(pl.BlockSpec(memory_space=pl.ANY),) * 2,
         scratch_shapes=[
+            pltpu.VMEM((12, 112), BF16),
+            pltpu.VMEM((MINE, 112, 2048), BF16),
+            dma((MINE + 1,)),
+            pltpu.VMEM((12, 112), BF16),
+            pltpu.VMEM((8, 12), jnp.int32),
+            pltpu.VMEM((8, 12), F32),
+            pltpu.VMEM((MINE, SLOTS, 112), BF16),
+            pltpu.VMEM((MINE, 112, 2048), BF16),
+            pltpu.VMEM((MINE, 112, 1024), BF16),
+            dma((8,)),
             pltpu.VMEM((128, 128), BF16),
             pltpu.VMEM((8, 128), jnp.int32),
             pltpu.VMEM((8, 128), F32),
@@ -268,7 +356,10 @@
             pltpu.VMEM((PEERS, 16, 128), BF16),
             pltpu.VMEM((MINE * SLOTS, 128), BF16),
             pltpu.VMEM((SIDE, MINE, 2 * SLOTS, 128), BF16),
-            pltpu.VMEM((MINE, SIDE - 1, 2 * SLOTS, 128), BF16),
+            pltpu.VMEM((MINE, 4, 2 * SLOTS, 128), BF16),
+            pltpu.VMEM((MINE, 2, 2 * SLOTS, 128), BF16),
+            pltpu.VMEM((MINE, 2, SLOTS, 128), BF16),
+            pltpu.VMEM((MINE, 2, 2 * SLOTS, 128), BF16),
             pltpu.VMEM((SIDE, MINE, SLOTS, 128), BF16),
             pltpu.VMEM((MINE, SIDE - 1, SLOTS, 128), BF16),
             pltpu.VMEM((SIDE, MINE, 24, 128), F32),
@@ -279,11 +370,12 @@
             pltpu.VMEM((PEERS, 16, 128), BF16),
             pltpu.VMEM((PEERS, 16, 128), BF16),
             dma((4,)),
-            dma((5, MINE)),
-            dma((5, MINE)),
+            dma((7, MINE)),
+            dma((7, MINE)),
+            pltpu.SemaphoreType.REGULAR((SIDE,)),
         ],
         compiler_params=pltpu.CompilerParams(
-            collective_id=1, has_side_effects=True, vmem_limit_bytes=48 << 20
+            collective_id=1, has_side_effects=True, vmem_limit_bytes=60 << 20
         ),
     )(
         output_grad,

time: 74.6 us -> 71.2 us (0.954)
  local copies, waits for them, and re-layouts: 6.96 us -> 3.84 us
    unnamed x14 -> x2, local copies, waits for them, and re-layouts: 6.96 us -> 3.84 us
where the time goes in v2:
time: 71.2 us; the launch traced here: 70.9 us
  Pallas kernels  66.5 us (93%)
  local copies, waits for them, and re-layouts  3.84 us (5%)
    pallas_call x1, Pallas kernels, body(): pl.pallas_call(kernel, out_shape=(jax.ShapeDtypeStruct(output_grad.shape,...  66.5 us
    unnamed x2, local copies, waits for them, and re-layouts  3.84 us

profile of v2, /device:TPU:1, one launch (start us, length us, event | category | flops | bytes accessed | tf_op | source)
XLA Modules:
  0.0 70.9 jit_solution(18255181932502200575)
XLA Ops:
  0.6 66.5 %shard_map.77 = (bf16[12,112]{1,0:T(8,128)(2,1)}, bf16[3,112,2048]{2,1,0:T(8,128)(2,1)}) custom-call(bf16[12,112]{1,0:T(8,128)(2,1)} %og_hbm.1, s32[8,12]{1,0:T(8,128)} %bitcast.4, f32[8,12]{1,0:T(8,128)} %bitcast.5, bf16[3,64,112]{2,1,0:T(8,128)(2,1)} %x_hbm.1, bf16[3,112,2048]{2,1,0:T(8,128)(2,1)} %w_hbm.1, bf16[3,112,1024]{2,1,0:T(8,128)(2,1)} %bitcast.3), custom_call_target="tpu_custom_call" | custom-call | tf_op jit(solution)/shard_map/pallas_call | solution.py:332
  67.1 1.3 %copy.10 = bf16[12,112]{1,0:T(8,128)(2,1)} copy(bf16[12,112]{1,0:T(8,128)(2,1)} %get-tuple-element.4) | data formatting | bytes 5376
  68.4 2.6 %copy.11 = bf16[3,112,2048]{2,1,0:T(8,128)(2,1)} copy(bf16[3,112,2048]{2,1,0:T(8,128)(2,1)} %get-tuple-element.5) | data formatting | bytes 2752512

commit v3 on v2

--- a/solution.py
+++ b/solution.py
@@ -16,8 +16,7 @@
 
 def kernel(
     og_hbm, rt_hbm, gt_hbm, x_hbm, w_hbm, d_hbm,
-    ig_hbm, wg_hbm,
-    ig_ref, wg_ref, out_sems,
+    ig_ref, wg_ref,
     og_ref, rt_ref, gt_ref, x_ref, w_ref, d_ref, in_sems,
     og_pad, rt_pad, gt_pad, table,
     e1_send, e1_recv, got, gu_send, gu_recv, far3, far4, passed, h_send, h_recv, s2_send, s2_recv,
@@ -253,9 +252,10 @@
     for e in range(MINE):
         wait(gath.at[e, 0, 0 : SIDE - 1], r_sems.at[3, e])
 
-        @pl.loop(1, SIDE)
-        def _(k):
-            device, _to = along_first(k)
+        @pl.loop(0, SIDE - 1)
+        def _(k):
+            skip = jnp.where(k >= z, k + 1, k) - z
+            device, _to = along_first(jnp.where(even, k + 1, skip + SIDE))
             here = gath.at[e, first]
             send(here, here, s_sems.at[4, e], r_sems.at[4, e], device)
 
@@ -299,7 +299,6 @@
             wg_ref[e, :, cols] = lax.dot_general(
                 x_ref[e], pre[e, :, cols], (((0,), (0,)), ((), ())), preferred_element_type=F32
             ).astype(BF16)
-        pltpu.make_async_copy(wg_ref.at[e], wg_hbm.at[e], out_sems.at[e]).start()
 
     wait(e2_recv.at[0 : PEERS - 1], e_sems.at[3])
     token = lax.dot_general(
@@ -309,12 +308,7 @@
         preferred_element_type=F32,
     )
     ig_ref[...] = token[0:12, 0:112].astype(BF16)
-    last = pltpu.make_async_copy(ig_ref, ig_hbm, out_sems.at[MINE])
-    last.start()
-
-    for e in range(MINE):
-        pltpu.make_async_copy(wg_ref.at[e], wg_hbm.at[e], out_sems.at[e]).wait()
-    last.wait()
+
     wait(e1_send.at[0 : PEERS - 1], e_sems.at[0])
     wait(e2_send.at[0 : PEERS - 1], e_sems.at[2])
     for e in range(MINE):
@@ -335,12 +329,9 @@
             jax.ShapeDtypeStruct(output_grad.shape, BF16),
             jax.ShapeDtypeStruct(gate_up.shape, BF16),
         ),
-        in_specs=[pl.BlockSpec(memory_space=pl.ANY)] * 6,
-        out_specs=(pl.BlockSpec(memory_space=pl.ANY),) * 2,
+        in_specs=[pl.BlockSpec(memory_space=pltpu.HBM)] * 6,
+        out_specs=(pl.BlockSpec(memory_space=pltpu.VMEM),) * 2,
         scratch_shapes=[
-            pltpu.VMEM((12, 112), BF16),
-            pltpu.VMEM((MINE, 112, 2048), BF16),
-            dma((MINE + 1,)),
             pltpu.VMEM((12, 112), BF16),
             pltpu.VMEM((8, 12), jnp.int32),
             pltpu.VMEM((8, 12), F32),
@@ -375,15 +366,16 @@
             pltpu.SemaphoreType.REGULAR((SIDE,)),
         ],
         compiler_params=pltpu.CompilerParams(
-            collective_id=1, has_side_effects=True, vmem_limit_bytes=60 << 20
+            collective_id=1, has_side_effects=True, vmem_limit_bytes=24 << 20
         ),
     )(
-        output_grad,
-        routing.T,
-        gates.T,
-        saved_inputs,
-        gate_up,
-        jnp.swapaxes(down_weight, 1, 2),
+        *(
+            pltpu.with_memory_space_constraint(v, pltpu.HBM)
+            for v in (
+                output_grad, routing.T, gates.T, saved_inputs, gate_up,
+                jnp.swapaxes(down_weight, 1, 2),
+            )
+        )
     )
 
 

time: 71.2 us -> 66.8 us (0.938)
  Pallas kernels: 66.5 us -> 64.3 us
  local copies, waits for them, and re-layouts: 3.84 us -> 1.67 us
    unnamed x2, local copies, waits for them, and re-layouts: 3.84 us -> 1.67 us
    pallas_call x1, Pallas kernels: 66.5 us -> 64.3 us  [body(): pl.pallas_call(kernel, out_shape=(jax.ShapeDtypeStruct(output_grad.shape,...]
where the time goes in v3:
time: 66.8 us; the launch traced here: 66.7 us
  Pallas kernels  64.3 us (96%)
  local copies, waits for them, and re-layouts  1.67 us (2%)
    pallas_call x1, Pallas kernels, body(): pl.pallas_call(kernel, out_shape=(jax.ShapeDtypeStruct(output_grad.shape,...  64.3 us
    unnamed x2, local copies, waits for them, and re-layouts  1.67 us

profile of v3, /device:TPU:1, one launch (start us, length us, event | category | flops | bytes accessed | tf_op | source)
XLA Modules:
  0.0 66.7 jit_solution(10233207446103354599)
XLA Ops:
  0.6 64.3 %shard_map.77 = (bf16[12,112]{1,0:T(8,128)(2,1)S(1)}, bf16[3,112,2048]{2,1,0:T(8,128)(2,1)S(1)}) custom-call(bf16[12,112]{1,0:T(8,128)(2,1)} %og_hbm.1, s32[8,12]{1,0:T(8,128)} %bitcast.4, f32[8,12]{1,0:T(8,128)} %bitcast.5, bf16[3,64,112]{2,1,0:T(8,128)(2,1)} %x_hbm.1, bf16[3,112,2048]{2,1,0:T(8,128)(2,1)} %w_hbm.1, bf16[3,112,1024]{2,1,0:T(8,128)(2,1)} %bitcast.3), custom_call_target="tpu_custom_call" | custom-call | tf_op jit(solution)/shard_map/pallas_call | solution.py:326
  65.0 0.6 copy.10
  65.6 1.1 %copy.11 = bf16[3,112,2048]{2,1,0:T(8,128)(2,1)} copy(bf16[3,112,2048]{2,1,0:T(8,128)(2,1)S(1)} %get-tuple-element.5) | data formatting | bytes 2752512
